TPU v7x, 32 devices: a whole 2x2x4 slice. The times are simulated.
32 devices in a mesh: parts: 2 (over x), sec: 16 (over z, y, core).
Axes of the slice: x: 2, y: 2, z: 4, core: 2. Of those that a mesh axis runs over, the one named last changes fastest.
Arguments:
- left_env: float32 [128, 13, 128, 128], P(('parts', 'sec')), parts along dimension 0, as said below
- right_env: float32 [128, 13, 128, 128], P(('parts', 'sec')), parts along dimension 0, as said below
- hop_ops: float32 [128, 4, 128, 128], P(('parts', 'sec')), parts along dimension 0, may hold values from -0.5 to 0.5
- start: float32 [128, 128, 128], P(('parts', 'sec')), parts along dimension 0, may hold values from -6 to 6
- left_dims: int32 [128], P(('parts', 'sec')), parts along dimension 0, may hold values from 32 to 128, as said below
- right_dims: int32 [128], P(('parts', 'sec')), parts along dimension 0, may hold values from 32 to 128, as said below
Outputs:
- ritz: float32 [128, 128, 128], P(('parts', 'sec')), parts along dimension 0
- energy: float32 [2], P('parts'), parts along dimension 0
There are 2 independent parts, one for each index of `parts`. A program takes and returns all parts, laid end to end along the dimension named above; each array names one. Nothing has to cross between parts.
Inputs may be any that keep to these rules, and one draw needn't show every extreme that they name: `left_dims`: live rows of a sector; some sector has all 128. `right_dims`: live columns of a sector; some sector has all 128. `left_env`: each block is symmetric. `right_env`: each block is symmetric.
All inputs are finite; a program needn't handle non-finite values.
Results may differ from a plain program's by a relative error of at most 0.0001.
Values sent between devices are 32-bit elements; how exact they have to be, the bound alone decides.
A program may use at most 64 MiB of HBM per device.

v0:
```python
import jax
import jax.numpy as jnp
from jax import lax
from jax.sharding import PartitionSpec as P

ITERS = 4


highest = lax.Precision.HIGHEST
epsilon = 1e-12


def shifted(shard, axis, by):
    peers = lax.axis_size(axis)
    pairs = [(i, i + by) for i in range(peers) if 0 <= i + by < peers]
    return lax.ppermute(shard, axis, pairs)


def with_halo(shard, sides, width):
    for axis, dim in sides:
        peers, length = (lax.axis_size(axis), shard.shape[dim])
        up = [(i, (i + 1) % peers) for i in range(peers - 1)]
        down = [(j, i) for i, j in up]
        last = lax.slice_in_dim(shard, length - width, length, axis=dim)
        initial = lax.slice_in_dim(shard, 0, width, axis=dim)
        before = lax.ppermute(last, axis, up)
        after = lax.ppermute(initial, axis, down)
        shard = jnp.concatenate([before, shard, after], axis=dim)
    return shard


def diagonal_terms(left_env, right_env, blocks):
    partial_left = jnp.einsum("swab,sbc->swac", left_env, blocks, precision=highest)
    return jnp.einsum("swac,swcd->sad", partial_left, right_env, precision=highest)


def forward_term(hop_ops, blocks, offset):
    first = 2 * offset - 2
    partial_left = jnp.einsum("sab,sbc->sac", hop_ops[:, first], blocks, precision=highest)
    return jnp.einsum("sac,scd->sad", partial_left, hop_ops[:, first + 1], precision=highest)


def backward_term(hop_ops, blocks, offset):
    first = 2 * offset - 2
    partial_left = jnp.einsum("sba,sbc->sac", hop_ops[:, first], blocks, precision=highest)
    return jnp.einsum("sac,sdc->sad", partial_left, hop_ops[:, first + 1], precision=highest)


def on_device(left_env, right_env, hop_ops, start, left_dims, right_dims):
    count = start.shape[0]
    block_size = start.shape[1]
    positions = jnp.arange(block_size, dtype=jnp.int32)
    row_live = positions[None, :] < left_dims[:, None]
    col_live = positions[None, :] < right_dims[:, None]
    live_mask = (row_live[:, :, None] & col_live[:, None, :]).astype(jnp.float32)
    rim_ops = shifted(hop_ops[-2:], "sec", 1)
    ops_extended = jnp.concatenate([rim_ops, hop_ops], 0)

    def coupling(blocks):
        extended = with_halo(blocks, (("sec", 0),), 2)
        total = jnp.zeros_like(blocks)
        for offset in (1, 2):
            total = total + forward_term(hop_ops, extended[2 + offset : 2 + offset + count], offset)
            total = total + backward_term(
                ops_extended[2 - offset : 2 - offset + count],
                extended[2 - offset : 2 - offset + count],
                offset,
            )
        return total

    def apply_hamiltonian(blocks):
        return live_mask * (diagonal_terms(left_env, right_env, blocks) + coupling(blocks))

    masked = live_mask * start
    lowest = jnp.float32(0.0)
    start_sq = lax.psum(jnp.sum(masked * masked), "sec")
    current = masked / jnp.sqrt(start_sq)
    image = apply_hamiltonian(current)
    for iteration in range(ITERS):
        rayleigh = lax.psum(jnp.sum(current * image), "sec")
        residual = image - rayleigh * current
        res_sq = lax.psum(jnp.sum(residual * residual), "sec")
        res_norm = jnp.sqrt(res_sq + epsilon)
        direction = residual / res_norm
        bent = apply_hamiltonian(direction)
        curvature = lax.psum(jnp.sum(direction * bent), "sec")
        lowest = (rayleigh + curvature) / 2 - jnp.sqrt(
            ((rayleigh - curvature) / 2) ** 2 + res_norm * res_norm
        )
        slope = lowest - rayleigh
        length = jnp.sqrt(res_norm * res_norm + slope * slope)
        current = (res_norm * current + slope * direction) / length
        image = (res_norm * image + slope * bent) / length
    total_entries = count * lax.axis_size("sec") * block_size * block_size
    ritz = current * jnp.sqrt(jnp.float32(total_entries))
    return (ritz, jnp.reshape(lowest, (1,)))


def solution(mesh):
    in_specs = (
        P(("parts", "sec"), None, None, None),
        P(("parts", "sec"), None, None, None),
        P(("parts", "sec"), None, None, None),
        P(("parts", "sec"), None, None),
        P(("parts", "sec")),
        P(("parts", "sec")),
    )
    out_specs = (P(("parts", "sec"), None, None), P("parts"))
    return jax.shard_map(
        on_device, mesh=mesh, in_specs=in_specs, out_specs=out_specs, check_vma=False
    )
```

profile of v0, /device:TPU:0, one launch (start us, length us, event | category | flops | bytes accessed | tf_op | source)
XLA Modules:
  0.0 558.6 jit_solution(9601404614392264343)
XLA Ops:
  3.4 35.5 %psum.91 = f32[]{:T(128)} all-reduce(f32[]{:T(128)} %multiply_reduce_fusion.11), channel_id=1, replica_groups=mesh['parts'=2,'sec'=16] {'sec'}, use_global_device_ids=true, to_apply=%region_1.0 | all-reduce | flops 1 | bytes 8 | tf_op jit(solution)/shard_map/psum | solution.py:76
  42.0 3.0 collective-permute-start.2
  48.4 2.9 fusion.80
  51.4 3.4 fusion.10
  60.4 30.1 %psum.92 = f32[]{:T(128)} all-reduce(f32[]{:T(128)} %get-tuple-element.21), channel_id=1, replica_groups=mesh['parts'=2,'sec'=16] {'sec'}, use_global_device_ids=true, to_apply=%region_3.0 | all-reduce | flops 1 | bytes 8 | tf_op jit(solution)/shard_map/psum | solution.py:80
  93.0 30.6 %psum.93 = f32[]{:T(128)} all-reduce(f32[]{:T(128)} %multiply_reduce_fusion.9), channel_id=1, replica_groups=mesh['parts'=2,'sec'=16] {'sec'}, use_global_device_ids=true, to_apply=%region_5.0 | all-reduce | flops 1 | bytes 8 | tf_op jit(solution)/shard_map/psum | solution.py:82
  126.1 2.9 fusion.78
  131.0 4.1 fusion.13
  135.2 3.2 collective-permute-start.4
  146.7 3.0 multiply_reduce_fusion.8
  149.7 31.3 %psum.94 = f32[]{:T(128)} all-reduce(f32[]{:T(128)} %get-tuple-element.23), channel_id=1, replica_groups=mesh['parts'=2,'sec'=16] {'sec'}, use_global_device_ids=true, to_apply=%region_7.0 | all-reduce | flops 1 | bytes 8 | tf_op jit(solution)/shard_map/psum | solution.py:86
  184.4 2.7 multiply_reduce_fusion.7
  187.1 30.1 %psum.95 = f32[]{:T(128)} all-reduce(f32[]{:T(128)} %get-tuple-element.8), channel_id=1, replica_groups=mesh['parts'=2,'sec'=16] {'sec'}, use_global_device_ids=true, to_apply=%region_9.0 | all-reduce | flops 1 | bytes 8 | tf_op jit(solution)/shard_map/psum | solution.py:80
  219.6 30.3 %psum.96 = f32[]{:T(128)} all-reduce(f32[]{:T(128)} %multiply_reduce_fusion.6), channel_id=1, replica_groups=mesh['parts'=2,'sec'=16] {'sec'}, use_global_device_ids=true, to_apply=%region_11.0 | all-reduce | flops 1 | bytes 8 | tf_op jit(solution)/shard_map/psum | solution.py:82
  252.3 2.9 fusion.76
  257.2 4.1 fusion.16
  261.4 3.2 collective-permute-start.6
  273.0 3.0 multiply_reduce_fusion.5
  275.9 31.3 %psum.97 = f32[]{:T(128)} all-reduce(f32[]{:T(128)} %get-tuple-element.25), channel_id=1, replica_groups=mesh['parts'=2,'sec'=16] {'sec'}, use_global_device_ids=true, to_apply=%region_13.0 | all-reduce | flops 1 | bytes 8 | tf_op jit(solution)/shard_map/psum | solution.py:86
  313.2 30.1 %psum.98 = f32[]{:T(128)} all-reduce(f32[]{:T(128)} %get-tuple-element.5), channel_id=1, replica_groups=mesh['parts'=2,'sec'=16] {'sec'}, use_global_device_ids=true, to_apply=%region_15.0 | all-reduce | flops 1 | bytes 8 | tf_op jit(solution)/shard_map/psum | solution.py:80
  345.6 30.3 %psum.99 = f32[]{:T(128)} all-reduce(f32[]{:T(128)} %multiply_reduce_fusion.3), channel_id=1, replica_groups=mesh['parts'=2,'sec'=16] {'sec'}, use_global_device_ids=true, to_apply=%region_17.0 | all-reduce | flops 1 | bytes 8 | tf_op jit(solution)/shard_map/psum | solution.py:82
  378.3 2.9 fusion.74
  383.2 4.1 fusion.19
  387.4 3.2 collective-permute-start.8
  399.0 3.0 multiply_reduce_fusion.2
  401.9 31.2 %psum.100 = f32[]{:T(128)} all-reduce(f32[]{:T(128)} %get-tuple-element.27), channel_id=1, replica_groups=mesh['parts'=2,'sec'=16] {'sec'}, use_global_device_ids=true, to_apply=%region_19.0 | all-reduce | flops 1 | bytes 8 | tf_op jit(solution)/shard_map/psum | solution.py:86
  439.1 30.1 %psum.101 = f32[]{:T(128)} all-reduce(f32[]{:T(128)} %get-tuple-element.2), channel_id=1, replica_groups=mesh['parts'=2,'sec'=16] {'sec'}, use_global_device_ids=true, to_apply=%region_21.0 | all-reduce | flops 1 | bytes 8 | tf_op jit(solution)/shard_map/psum | solution.py:80
  471.5 30.4 %psum.102 = f32[]{:T(128)} all-reduce(f32[]{:T(128)} %multiply_reduce_fusion), channel_id=1, replica_groups=mesh['parts'=2,'sec'=16] {'sec'}, use_global_device_ids=true, to_apply=%region_23.0 | all-reduce | flops 1 | bytes 8 | tf_op jit(solution)/shard_map/psum | solution.py:82
  504.2 2.9 fusion.72
  508.6 3.4 fusion.22
  512.0 3.0 collective-permute-start.10
  520.0 32.2 %psum.103 = f32[]{:T(128)} all-reduce(f32[]{:T(128)} %fusion.36), channel_id=1, replica_groups=mesh['parts'=2,'sec'=16] {'sec'}, use_global_device_ids=true, to_apply=%region_25.0 | all-reduce | flops 1 | bytes 8 | tf_op jit(solution)/shard_map/psum | solution.py:86
  (123 shorter events, 74.8 us)
Async XLA Ops:
  0.6 47.8 %copy-start = (f32[4,13,128,128]{3,2,1,0:T(8,128)S(1)}, f32[4,13,128,128]{3,2,1,0:T(8,128)}, u32[]{:S(2)}) copy-start(f32[4,13,128,128]{3,2,1,0:T(8,128)} %param.6) | copy-start | bytes 10223620
  40.7 14.1 %collective-permute-start = (f32[2,128,128]{2,1,0:T(8,128)S(1)}, f32[2,128,128]{2,1,0:T(8,128)S(1)}, u32[]{:S(2)}, u32[]{:S(2)}) collective-permute-start(f32[2,128,128]{2,1,0:T(8,128)S(1)} %get-tuple-element.20), channel_id=1, source_target_pairs={{1,0},{2,1},{3,2},{4,3},{5,4},{6,5},{7,6},{8,7},{9,8},{10,9},{11,1... | collective-permute-start | bytes 393224 | tf_op jit(solution)/shard_map/ppermute | solution.py:27
  42.0 14.1 %collective-permute-start.2 = (f32[2,128,128]{2,1,0:T(8,128)S(1)}, f32[2,128,128]{2,1,0:T(8,128)S(1)}, u32[]{:S(2)}, u32[]{:S(2)}) collective-permute-start(f32[2,128,128]{2,1,0:T(8,128)S(1)} %get-tuple-element.19), channel_id=1, source_target_pairs={{0,1},{1,2},{2,3},{3,4},{4,5},{5,6},{6,7},{7,8},{8,9},{9,10},{10,1... | collective-permute-start | bytes 393224 | tf_op jit(solution)/shard_map/ppermute | solution.py:26
  46.2 5.1 copy-start.1
  46.2 9.8 %collective-permute-start.1 = (f32[2,4,128,128]{3,2,0,1:T(8,128)S(1)}, f32[2,4,128,128]{3,2,0,1:T(8,128)S(1)}, u32[]{:S(2)}, u32[]{:S(2)}) collective-permute-start(f32[2,4,128,128]{3,2,0,1:T(8,128)S(1)} %copy.53), channel_id=1, source_target_pairs={{0,1},{1,2},{2,3},{3,4},{4,5},{5,6},{6,7},{7,8},{8,9},{9,10},{10,1... | collective-permute-start | bytes 1572872 | tf_op jit(solution)/shard_map/ppermute | solution.py:16
  51.4 3.5 copy-start.6
  126.0 5.0 copy-start.2
  129.7 8.6 %collective-permute-start.3 = (f32[2,128,128]{2,1,0:T(8,128)}, f32[2,128,128]{2,1,0:T(8,128)S(1)}, u32[]{:S(2)}, u32[]{:S(2)}) collective-permute-start(f32[2,128,128]{2,1,0:T(8,128)} %get-tuple-element.18), channel_id=1, source_target_pairs={{1,0},{2,1},{3,2},{4,3},{5,4},{6,5},{7,6},{8,7},{9,8},{10,9},{11,1... | collective-permute-start | bytes 393224 | tf_op jit(solution)/shard_map/ppermute | solution.py:27
  135.1 9.2 %copy-start.7 = (f32[4,4,128,128]{3,2,1,0:T(8,128)S(1)}, f32[4,4,128,128]{3,2,1,0:T(8,128)}, u32[]{:S(2)}) copy-start(f32[4,4,128,128]{3,2,1,0:T(8,128)} %param.8) | copy-start | bytes 3145732
  135.1 9.2 %copy-start.12 = (f32[4,128,128]{2,1,0:T(8,128)S(1)}, f32[4,128,128]{2,1,0:T(8,128)}, u32[]{:S(2)}) copy-start(f32[4,128,128]{2,1,0:T(8,128)} %copy-done.11) | copy-start | bytes 786436
  135.1 11.6 %copy-start.20 = (f32[4,128,128]{2,1,0:T(8,128)S(1)}, f32[4,128,128]{2,1,0:T(8,128)}, u32[]{:S(2)}) copy-start(f32[4,128,128]{2,1,0:T(8,128)} %fusion.13) | copy-start | bytes 786436
  135.2 6.0 %collective-permute-start.4 = (f32[2,128,128]{2,1,0:T(8,128)}, f32[2,128,128]{2,1,0:T(8,128)S(1)}, u32[]{:S(2)}, u32[]{:S(2)}) collective-permute-start(f32[2,128,128]{2,1,0:T(8,128)} %get-tuple-element.17), channel_id=1, source_target_pairs={{0,1},{1,2},{2,3},{3,4},{4,5},{5,6},{6,7},{7,8},{8,9},{9,10},{10,1... | collective-permute-start | bytes 393224 | tf_op jit(solution)/shard_map/ppermute | solution.py:26
  252.3 2.9 copy-start.13
  252.3 4.9 copy-start.3
  255.9 8.6 %collective-permute-start.5 = (f32[2,128,128]{2,1,0:T(8,128)}, f32[2,128,128]{2,1,0:T(8,128)S(1)}, u32[]{:S(2)}, u32[]{:S(2)}) collective-permute-start(f32[2,128,128]{2,1,0:T(8,128)} %get-tuple-element.16), channel_id=1, source_target_pairs={{1,0},{2,1},{3,2},{4,3},{5,4},{6,5},{7,6},{8,7},{9,8},{10,9},{11,1... | collective-permute-start | bytes 393224 | tf_op jit(solution)/shard_map/ppermute | solution.py:27
  261.4 9.2 %copy-start.8 = (f32[4,4,128,128]{3,2,1,0:T(8,128)S(1)}, f32[4,4,128,128]{3,2,1,0:T(8,128)}, u32[]{:S(2)}) copy-start(f32[4,4,128,128]{3,2,1,0:T(8,128)} %param.8) | copy-start | bytes 3145732
  261.4 9.2 %copy-start.14 = (f32[4,128,128]{2,1,0:T(8,128)S(1)}, f32[4,128,128]{2,1,0:T(8,128)}, u32[]{:S(2)}) copy-start(f32[4,128,128]{2,1,0:T(8,128)} %copy-done.13) | copy-start | bytes 786436
  261.4 11.6 %copy-start.21 = (f32[4,128,128]{2,1,0:T(8,128)S(1)}, f32[4,128,128]{2,1,0:T(8,128)}, u32[]{:S(2)}) copy-start(f32[4,128,128]{2,1,0:T(8,128)} %fusion.16) | copy-start | bytes 786436
  261.4 6.0 %collective-permute-start.6 = (f32[2,128,128]{2,1,0:T(8,128)}, f32[2,128,128]{2,1,0:T(8,128)S(1)}, u32[]{:S(2)}, u32[]{:S(2)}) collective-permute-start(f32[2,128,128]{2,1,0:T(8,128)} %get-tuple-element.15), channel_id=1, source_target_pairs={{0,1},{1,2},{2,3},{3,4},{4,5},{5,6},{6,7},{7,8},{8,9},{9,10},{10,1... | collective-permute-start | bytes 393224 | tf_op jit(solution)/shard_map/ppermute | solution.py:26
  378.3 2.9 copy-start.15
  378.3 4.9 copy-start.4
  381.9 8.6 %collective-permute-start.7 = (f32[2,128,128]{2,1,0:T(8,128)}, f32[2,128,128]{2,1,0:T(8,128)S(1)}, u32[]{:S(2)}, u32[]{:S(2)}) collective-permute-start(f32[2,128,128]{2,1,0:T(8,128)} %get-tuple-element.14), channel_id=1, source_target_pairs={{1,0},{2,1},{3,2},{4,3},{5,4},{6,5},{7,6},{8,7},{9,8},{10,9},{11,1... | collective-permute-start | bytes 393224 | tf_op jit(solution)/shard_map/ppermute | solution.py:27
  387.4 9.2 %copy-start.9 = (f32[4,4,128,128]{3,2,1,0:T(8,128)S(1)}, f32[4,4,128,128]{3,2,1,0:T(8,128)}, u32[]{:S(2)}) copy-start(f32[4,4,128,128]{3,2,1,0:T(8,128)} %param.8) | copy-start | bytes 3145732
  387.4 9.2 %copy-start.16 = (f32[4,128,128]{2,1,0:T(8,128)S(1)}, f32[4,128,128]{2,1,0:T(8,128)}, u32[]{:S(2)}) copy-start(f32[4,128,128]{2,1,0:T(8,128)} %copy-done.15) | copy-start | bytes 786436
  387.4 11.6 %copy-start.22 = (f32[4,128,128]{2,1,0:T(8,128)S(1)}, f32[4,128,128]{2,1,0:T(8,128)}, u32[]{:S(2)}) copy-start(f32[4,128,128]{2,1,0:T(8,128)} %fusion.19) | copy-start | bytes 786436
  387.4 6.0 %collective-permute-start.8 = (f32[2,128,128]{2,1,0:T(8,128)}, f32[2,128,128]{2,1,0:T(8,128)S(1)}, u32[]{:S(2)}, u32[]{:S(2)}) collective-permute-start(f32[2,128,128]{2,1,0:T(8,128)} %get-tuple-element.13), channel_id=1, source_target_pairs={{0,1},{1,2},{2,3},{3,4},{4,5},{5,6},{6,7},{7,8},{8,9},{9,10},{10,1... | collective-permute-start | bytes 393224 | tf_op jit(solution)/shard_map/ppermute | solution.py:26
  504.2 14.5 %copy-start.17 = (f32[4,128,128]{2,1,0:T(8,128)}, f32[4,128,128]{2,1,0:T(8,128)S(1)}, u32[]{:S(2)}) copy-start(f32[4,128,128]{2,1,0:T(8,128)S(1)} %broadcast_divide_fusion) | copy-start | bytes 786436
  504.2 4.4 copy-start.5
  507.1 8.0 %copy-start.10 = (f32[4,4,128,128]{3,2,1,0:T(8,128)S(1)}, f32[4,4,128,128]{3,2,1,0:T(8,128)}, u32[]{:S(2)}) copy-start(f32[4,4,128,128]{3,2,1,0:T(8,128)} %param.8) | copy-start | bytes 3145732
  507.1 8.9 %copy-start.19 = (f32[6,4,128,128]{3,2,0,1:T(8,128)S(1)}, f32[6,4,128,128]{3,2,0,1:T(8,128)}, u32[]{:S(2)}) copy-start(f32[6,4,128,128]{3,2,0,1:T(8,128)} %copy-done.18) | copy-start | bytes 4718596
  507.1 7.9 %collective-permute-start.9 = (f32[2,128,128]{2,1,0:T(8,128)S(1)}, f32[2,128,128]{2,1,0:T(8,128)S(1)}, u32[]{:S(2)}, u32[]{:S(2)}) collective-permute-start(f32[2,128,128]{2,1,0:T(8,128)S(1)} %get-tuple-element.12), channel_id=1, source_target_pairs={{1,0},{2,1},{3,2},{4,3},{5,4},{6,5},{7,6},{8,7},{9,8},{10,9},{11,1... | collective-permute-start | bytes 393224 | tf_op jit(solution)/shard_map/ppermute | solution.py:27
  512.0 4.0 collective-permute-start.10
  (2 other events, 5.2 us)
where the time goes:
time: 568 us; the launch traced here: 559 us
  blocking collectives  403 us (71%)
  matrix products  77.7 us (14%)
  other arithmetic  30 us (5%)
  starting transfers between devices  24.3 us (4%)
  between operations  19.5 us (3%)
    psum x4, blocking collectives, on_device(): curvature = lax.psum(jnp.sum(direction * bent), 'sec')  126 us
    psum x4, blocking collectives, on_device(): res_sq = lax.psum(jnp.sum(residual * residual), 'sec')  122 us
    psum x4, blocking collectives, on_device(): rayleigh = lax.psum(jnp.sum(current * image), 'sec')  120 us
    psum x1, blocking collectives, on_device(): start_sq = lax.psum(jnp.sum(masked * masked), 'sec')  35.5 us
    dot_general x5, matrix products, diagonal_terms(): jnp.einsum('swac,swcd->sad', partial_left, right_env, precision=highest)  19.2 us
    dot_general x10, matrix products, backward_term(): jnp.einsum('sac,sdc->sad', partial_left, hop_ops[:, first + 1], precision...  18.4 us
    ppermute x5, starting transfers between devices, with_halo(): before = lax.ppermute(last, axis, up)  15.5 us
    dot_general x5, matrix products, diagonal_terms(): jnp.einsum('swab,sbc->swac', left_env, blocks, precision=highest)  14.5 us
  transfers between devices with their start and end apart: 11, of which 1 were waited for; matrix products, arithmetic and copies ran while one was open for 6% of the time, Pallas kernels for 0%

commit v1 on v0

v1 whole, which is shorter than its diff:
```python
import functools
import math

import jax
import jax.numpy as jnp
from jax import lax
from jax.experimental import pallas as pl
from jax.experimental.pallas import tpu as pltpu
from jax.sharding import PartitionSpec as P

ITERS = 4
EPSILON = 1e-12
MESH = pl.DeviceIdType.MESH
f32 = jnp.float32
bf16 = jnp.bfloat16


def halves(x):
    hi = x.astype(bf16)
    return hi, (x - hi.astype(f32)).astype(bf16)


def fold(x):
    return jnp.sum(x, axis=0, keepdims=True)


def kernel(
    n, count, terms,
    left_env, right_env, hop_ops, start, left_dims, right_dims,
    ritz, energy,
    left_in, right_in, hop_in, rim, ops_left, ops_right, ops_halo, middle,
    cur, img, out, halo_in, halo_cur, halo_img, part, sums,
    load_sem, rim_send, rim_recv, halo_send, halo_recv, sum_send, sum_recv,
):
    size = start.shape[1]
    me = lax.axis_index("sec")
    has_left, has_right = me > 0, me < n - 1
    left, right = lax.max(me - 1, 0), lax.min(me + 1, n - 1)
    steps = ITERS + 1

    loads = [pltpu.make_async_copy(start, img, load_sem.at[0]),
             pltpu.make_async_copy(hop_ops, hop_in, load_sem.at[1])]
    for s in range(count):
        loads.append(pltpu.make_async_copy(left_env.at[s], left_in.at[s], load_sem.at[2 + 2 * s]))
        loads.append(pltpu.make_async_copy(right_env.at[s], right_in.at[s], load_sem.at[3 + 2 * s]))
    for load in loads:
        load.start()

    barrier = pltpu.get_barrier_semaphore()

    def greet(j, carry):
        pl.semaphore_signal(barrier, inc=1, device_id={"sec": lax.rem(me + j, n)}, device_id_type=MESH)
        return carry

    lax.fori_loop(1, n, greet, 0)

    rows = lax.broadcasted_iota(jnp.int32, (size, size), 0)
    cols = lax.broadcasted_iota(jnp.int32, (size, size), 1)

    def masked(s, x):
        return jnp.where((rows < left_dims[s]) & (cols < right_dims[s]), x, 0.0)

    zero = jnp.zeros((size, size), f32)
    halo_cur[...] = jnp.zeros_like(halo_cur)
    cur[...] = jnp.zeros_like(cur)

    @pl.when(jnp.logical_not(has_left))
    def _():
        rim[...] = jnp.zeros_like(rim)
        for p in range(steps):
            halo_in[p, 0:2] = jnp.zeros((2, size, size), f32)

    @pl.when(jnp.logical_not(has_right))
    def _():
        for p in range(steps):
            halo_in[p, 2:4] = jnp.zeros((2, size, size), f32)

    scale = 1.0 / (6.0 * math.sqrt(count * n * size * size))
    loads[0].wait()
    for s in range(count):
        img[s] = masked(s, img[s]) * scale

    pl.semaphore_wait(barrier, n - 1)

    def halo_copy(src, p, s, slot):
        device = right if slot < 2 else left
        return pltpu.make_async_remote_copy(
            src_ref=src.at[s], dst_ref=halo_in.at[p, slot],
            send_sem=halo_send.at[p, slot], recv_sem=halo_recv.at[p, slot],
            device_id={"sec": device}, device_id_type=MESH)

    targets = {}
    for i in range(2):
        targets.setdefault(count - 2 + i, []).append(i)
        targets.setdefault(i, []).append(2 + i)

    def halo_start(src, p, s, more=True):
        for slot in targets.get(s, ()):
            @pl.when((has_right if slot < 2 else has_left) & more)
            def _():
                halo_copy(src, p, s, slot).start()

    def halo_wait_send(src, p):
        for s in targets:
            for slot in targets[s]:
                @pl.when(has_right if slot < 2 else has_left)
                def _():
                    halo_copy(src, p, s, slot).wait_send()

    def halo_wait_recv(p):
        for slot in range(4):
            @pl.when(has_left if slot < 2 else has_right)
            def _():
                halo_copy(img, p, 0, slot).wait_recv()

    for s in range(count):
        halo_start(img, 0, s)
    rim_copy = pltpu.make_async_remote_copy(
        src_ref=hop_ops.at[count - 2:count], dst_ref=rim,
        send_sem=rim_send, recv_sem=rim_recv, device_id={"sec": right}, device_id_type=MESH)

    @pl.when(has_right)
    def _():
        rim_copy.start()

    def sum_start(which, p, partial):
        sums[which, p, me] = partial
        part[which] = partial

        def send(j, carry):
            pltpu.make_async_remote_copy(
                src_ref=part.at[which], dst_ref=sums.at[which, p, me],
                send_sem=sum_send.at[which, p], recv_sem=sum_recv.at[which, p],
                device_id={"sec": lax.rem(me + j, n)}, device_id_type=MESH).start()
            return carry

        lax.fori_loop(1, n, send, 0)

    def sum_wait(which, p):
        whole = sums.at[which, p, 0:n - 1]
        pltpu.make_async_copy(whole, whole, sum_recv.at[which, p]).wait()
        pltpu.make_async_copy(whole, whole, sum_send.at[which, p]).wait()
        lanes = jnp.sum(sums[which, p], axis=0)
        return jnp.sum(lanes, axis=1, keepdims=True)

    def put(ref, index, row, x):
        hi, lo = halves(x)
        ref[index, row * size:(row + 1) * size, 0:size] = hi
        ref[index, row * size:(row + 1) * size, size:2 * size] = lo

    hop_rows = [[] for _ in range(count)]
    halo_rows = [[] for _ in range(4)]
    for k in (1, 2):
        for s in range(count):
            t = s + k
            entry = (s, terms + k - 1, s, k, False)
            (hop_rows[t] if t < count else halo_rows[2 + t - count]).append(entry)
            t = s - k
            entry = (s, terms + k + 1, t, k, True)
            (hop_rows[t] if t >= 0 else halo_rows[2 + t]).append(entry)

    def hop(owner, index):
        return hop_in[owner, index] if owner >= 0 else rim[2 + owner, index]

    loads[1].wait()
    for s in range(count):
        loads[2 + 2 * s].wait()
        for w in range(terms):
            put(ops_left, s, w, left_in[s, w])
        for i, (_, _, owner, k, flip) in enumerate(hop_rows[s]):
            block = hop(owner, 2 * k - 2)
            put(ops_left, s, terms + i, block.T if flip else block)
        loads[3 + 2 * s].wait()
        for w in range(terms):
            put(ops_right, s, w, right_in[s, w])
        for k in (1, 2):
            put(ops_right, s, terms + k - 1, hop(s, 2 * k - 1))
            if s - k >= 0:
                put(ops_right, s, terms + k + 1, hop(s - k, 2 * k - 1).T)

    @pl.when(has_left)
    def _():
        rim_copy.wait_recv()

    @pl.when(has_right)
    def _():
        rim_copy.wait_send()

    for slot in range(4):
        for i, (_, _, owner, k, flip) in enumerate(halo_rows[slot]):
            block = hop(owner, 2 * k - 2)
            put(ops_halo, slot, i, block.T if flip else block)
    for s in range(count):
        for k in (1, 2):
            if s - k < 0:
                put(ops_right, s, terms + k + 1, hop(s - k, 2 * k - 1).T)

    halo_wait_recv(0)
    halo_wait_send(img, 0)
    halo_img[...] = halo_in[0]

    def first_stage(ops, index, x, targets_of):
        hi, lo = halves(x)
        line = jnp.concatenate([hi, lo], axis=1)
        both = jnp.concatenate([line, line], axis=0)
        chunk = 4
        for base in range(0, len(targets_of), chunk):
            some = targets_of[base:base + chunk]
            product = jnp.dot(ops[index, base * size:(base + len(some)) * size, :], both,
                              preferred_element_type=f32)
            for i, (s, column) in enumerate(some):
                y = product[i * size:(i + 1) * size]
                hi, lo = halves(y[:, :size] + y[:, size:])
                middle[s, 0:size, column * size:(column + 1) * size] = hi
                middle[s, size:2 * size, column * size:(column + 1) * size] = lo

    order = []
    for s in range((count + 1) // 2):
        order += [s] if s == count - 1 - s else [s, count - 1 - s]

    def step(p, carry):
        partial = jnp.zeros((size, size), f32)
        for s in range(count):
            partial += cur[s] * img[s]
        sum_start(0, p, jnp.concatenate([fold(partial)] * 2, axis=0))

        for t in range(count):
            first_stage(ops_left, t, img[t],
                        [(t, w) for w in range(terms)] + [(e[0], e[1]) for e in hop_rows[t]])
        for slot in range(4):
            first_stage(ops_halo, slot, halo_img[slot], [(e[0], e[1]) for e in halo_rows[slot]])
        for s in order:
            product = jnp.dot(middle[s], ops_right[s], preferred_element_type=f32)
            product = product[:size] + product[size:]
            out[s] = masked(s, product[:, :size] + product[:, size:])
            halo_start(out, p + 1, s, p < ITERS)

        rayleigh = sum_wait(0, p)[0:1]
        square = jnp.zeros((size, size), f32)
        bend = jnp.zeros((size, size), f32)
        for s in range(count):
            residual = img[s] - rayleigh * cur[s]
            square += residual * residual
            bend += residual * (out[s] - rayleigh * img[s])
        sum_start(1, p, jnp.concatenate([fold(square), fold(bend)], axis=0))
        both = sum_wait(1, p)
        first = p == 0
        res_sq = both[0:1] + EPSILON
        res_norm = jnp.sqrt(res_sq)
        curvature = both[1:2] / res_sq
        lowest = (rayleigh + curvature) / 2 - jnp.sqrt(((rayleigh - curvature) / 2) ** 2 + res_norm * res_norm)
        slope = lowest - rayleigh
        length = jnp.sqrt(res_norm * res_norm + slope * slope)
        keep = jnp.where(first, 0.0, res_norm / length)
        move = jnp.where(first, lax.rsqrt(both[0:1]), slope / length / res_norm)
        energy[...] = lowest

        for s in range(count):
            cur[s] = keep * cur[s] + move * (img[s] - rayleigh * cur[s])

        @pl.when(p < ITERS)
        def _():
            for s in range(count):
                img[s] = keep * img[s] + move * (out[s] - rayleigh * img[s])
            halo_wait_recv(p + 1)
            halo_wait_send(out, p + 1)
            for slot in range(4):
                halo_cur[slot], halo_img[slot] = (
                    keep * halo_cur[slot] + move * (halo_img[slot] - rayleigh * halo_cur[slot]),
                    keep * halo_img[slot] + move * (halo_in[p + 1, slot] - rayleigh * halo_img[slot]))

        return carry

    lax.fori_loop(0, steps, step, 0)
    ritz[...] = cur[...]


def on_device(left_env, right_env, hop_ops, start, left_dims, right_dims):
    count, terms, size = left_env.shape[0], left_env.shape[1], left_env.shape[2]
    n = lax.axis_size("sec")
    blocks = terms + 4
    steps = ITERS + 1
    dma = pltpu.SemaphoreType.DMA
    anywhere = pl.BlockSpec(memory_space=pl.ANY)
    scalars = pl.BlockSpec(memory_space=pltpu.SMEM)
    inside = pl.BlockSpec(memory_space=pltpu.VMEM)
    ritz, energy = pl.pallas_call(
        functools.partial(kernel, n, count, terms),
        out_shape=(jax.ShapeDtypeStruct((count, size, size), f32), jax.ShapeDtypeStruct((1, 1), f32)),
        in_specs=[anywhere] * 4 + [scalars] * 2,
        out_specs=(inside, inside),
        scratch_shapes=[
            pltpu.VMEM((count, terms, size, size), f32),
            pltpu.VMEM((count, terms, size, size), f32),
            pltpu.VMEM((count, 4, size, size), f32),
            pltpu.VMEM((2, 4, size, size), f32),
            pltpu.VMEM((count, blocks * size, 2 * size), bf16),
            pltpu.VMEM((count, blocks * size, 2 * size), bf16),
            pltpu.VMEM((4, 2 * size, 2 * size), bf16),
            pltpu.VMEM((count, 2 * size, blocks * size), bf16),
            pltpu.VMEM((count, size, size), f32),
            pltpu.VMEM((count, size, size), f32),
            pltpu.VMEM((count, size, size), f32),
            pltpu.VMEM((steps, 4, size, size), f32),
            pltpu.VMEM((4, size, size), f32),
            pltpu.VMEM((4, size, size), f32),
            pltpu.VMEM((2, 2, size), f32),
            pltpu.VMEM((2, steps, n, 2, size), f32),
            dma((2 + 2 * count,)),
            dma, dma,
            dma((steps, 4)), dma((steps, 4)),
            dma((2, steps)), dma((2, steps)),
        ],
        compiler_params=pltpu.CompilerParams(
            collective_id=0, has_side_effects=True, vmem_limit_bytes=48 * 1024 * 1024),
    )(left_env, right_env, hop_ops, start, left_dims, right_dims)
    total_entries = count * n * size * size
    return ritz * jnp.sqrt(jnp.float32(total_entries)), jnp.reshape(energy, (1,))


def solution(mesh):
    in_specs = (
        P(("parts", "sec"), None, None, None),
        P(("parts", "sec"), None, None, None),
        P(("parts", "sec"), None, None, None),
        P(("parts", "sec"), None, None),
        P(("parts", "sec")),
        P(("parts", "sec")),
    )
    out_specs = (P(("parts", "sec"), None, None), P("parts"))
    return jax.shard_map(
        on_device, mesh=mesh, in_specs=in_specs, out_specs=out_specs, check_vma=False
    )
```

time: 568 us -> 71.8 us (0.13); the launches traced: 559 us -> 71.5 us
  blocking collectives: 403 us -> 0 us
  matrix products: 77.7 us -> 0 us
  Pallas kernels: 0 us -> 63 us
  other arithmetic: 30 us -> 0.72 us
  starting transfers between devices: 24.3 us -> 0 us
  between operations: 19.5 us -> 2.34 us
    psum x13 -> x0, blocking collectives: 403 us -> none  [the longest x4 126 us: on_device(): curvature = lax.psum(jnp.sum(direction * bent), 'sec')]
    dot_general x50 -> x0, matrix products: 77.7 us -> none  [the longest x5 19.2 us: diagonal_terms(): jnp.einsum('swac,swcd->sad', partial_left, right_env, precision=highest)]
    pallas_call x0 -> x1, Pallas kernels: none -> 63 us  [on_device(): pl.pallas_call(functools.partial(kernel, n, count, terms), out_shape=(jax...]
    ppermute x11 -> x0, starting transfers between devices: 24.3 us -> none  [the longest x5 15.5 us: with_halo(): before = lax.ppermute(last, axis, up)]
    reduce_sum x8 -> x0, other arithmetic: 19.4 us -> none  [the longest x4 9.46 us: on_device(): res_sq = lax.psum(jnp.sum(residual * residual), 'sec')]
    div x5 -> x0, other arithmetic: 7.96 us -> none  [the longest x4 6.87 us: on_device(): direction = residual / res_norm]
  transfers between devices with their start and end apart: 11 -> 0, of which waited for: 1 -> 0; matrix products, arithmetic and copies ran while one was open for 6% -> 0% of each run, Pallas kernels for 0% -> 0%
where the time goes in v1:
time: 71.8 us; the launch traced here: 71.5 us
  Pallas kernels  63 us (88%)
  local copies, waits for them, and re-layouts  5.44 us (8%)
  between operations  2.34 us (3%)
  other arithmetic  0.72 us (1%)
    pallas_call x1, Pallas kernels, on_device(): pl.pallas_call(functools.partial(kernel, n, count, terms), out_shape=(jax...  63 us
    unnamed x10, local copies, waits for them, and re-layouts  5.44 us

profile of v1, /device:TPU:0, one launch (start us, length us, event | category | flops | bytes accessed | tf_op | source)
XLA Modules:
  0.0 71.5 jit_solution(16942542451082149906)
XLA Ops:
  0.6 0.0 copy-start
  0.6 2.0 %copy-done = f32[4,13,128,128]{3,2,1,0:T(8,128)S(1)} copy-done((f32[4,13,128,128]{3,2,1,0:T(8,128)S(1)}, f32[4,13,128,128]{3,2,1,0:T(8,128)}, u32[]{:S(2)}) %copy-start) | copy-done | bytes 3407896
  2.6 0.0 copy-start.1
  2.6 1.2 %copy-done.1 = f32[4,4,128,128]{3,2,1,0:T(8,128)S(1)} copy-done((f32[4,4,128,128]{3,2,1,0:T(8,128)S(1)}, f32[4,4,128,128]{3,2,1,0:T(8,128)}, u32[]{:S(2)}) %copy-start.1) | copy-done | bytes 1048600
  3.8 0.0 copy-start.2
  3.8 0.9 %copy-done.2 = f32[4,128,128]{2,1,0:T(8,128)S(1)} copy-done((f32[4,128,128]{2,1,0:T(8,128)S(1)}, f32[4,128,128]{2,1,0:T(8,128)}, u32[]{:S(2)}) %copy-start.2) | copy-done | bytes 262168
  4.8 0.0 copy-start.3
  4.8 0.7 copy-done.3
  5.4 0.0 copy-start.4
  5.4 0.7 copy-done.4
  6.1 63.0 %shard_map.77 = (f32[4,128,128]{2,1,0:T(8,128)S(1)}, f32[1,1]{1,0:T(1,128)}) custom-call(f32[4,13,128,128]{3,2,1,0:T(8,128)S(1)} %copy-done, f32[4,13,128,128]{3,2,1,0:T(8,128)} %right_env.1, f32[4,4,128,128]{3,2,1,0:T(8,128)S(1)} %copy-done.1, f32[4,128,128]{2,1,0:T(8,128)S(1)} %copy-done.2, s32[4]{0:T(128)S(1)} %copy-done.3, s32[4]{0:T(128)S(1)} %copy-done.4), custom_call_target="tpu_custom_call" | custom-call | tf_op jit(solution)/shard_map/pallas_call | solution.py:287
  69.1 0.7 %broadcast_multiply_fusion = f32[4,128,128]{2,1,0:T(8,128)} fusion(f32[4,128,128]{2,1,0:T(8,128)S(1)} %get-tuple-element.4), kind=kLoop, calls=%fused_computation | loop fusion | flops 65536 | bytes 524288 | tf_op jit(solution)/shard_map/mul | solution.py:318
Async XLA Ops:
  0.6 2.0 %copy-start = (f32[4,13,128,128]{3,2,1,0:T(8,128)S(1)}, f32[4,13,128,128]{3,2,1,0:T(8,128)}, u32[]{:S(2)}) copy-start(f32[4,13,128,128]{3,2,1,0:T(8,128)} %left_env.1) | copy-start | bytes 10223620
  2.6 1.2 %copy-start.1 = (f32[4,4,128,128]{3,2,1,0:T(8,128)S(1)}, f32[4,4,128,128]{3,2,1,0:T(8,128)}, u32[]{:S(2)}) copy-start(f32[4,4,128,128]{3,2,1,0:T(8,128)} %hop_ops.1) | copy-start | bytes 3145732
  3.8 0.9 %copy-start.2 = (f32[4,128,128]{2,1,0:T(8,128)S(1)}, f32[4,128,128]{2,1,0:T(8,128)}, u32[]{:S(2)}) copy-start(f32[4,128,128]{2,1,0:T(8,128)} %start.1) | copy-start | bytes 786436
  4.8 0.7 copy-start.3
  5.4 0.7 copy-start.4

commit v2 on v1

v2 whole, which is shorter than its diff:
```python
import functools
import math

import jax
import jax.numpy as jnp
from jax import lax
from jax.experimental import pallas as pl
from jax.experimental.pallas import tpu as pltpu
from jax.sharding import PartitionSpec as P

ITERS = 4
EPSILON = 1e-12
MESH = pl.DeviceIdType.MESH
f32 = jnp.float32
bf16 = jnp.bfloat16


def halves(x):
    hi = x.astype(bf16)
    return hi, (x - hi.astype(f32)).astype(bf16)


def kernel(
    n, count, terms,
    left_env, right_env, hop_ops, start, left_dims, right_dims,
    ritz, energy,
    left_in, right_in, hop_in, rim, ops_left, ops_right, ops_halo, middle,
    cur, img, top, own, out, halo_in, halo_top, sums, tops, coef,
    load_sem, rim_send, rim_recv, halo_send, halo_recv, sum_send, sum_recv,
):
    size = start.shape[1]
    me = lax.axis_index("sec")
    has_left, has_right = me > 0, me < n - 1
    left, right = lax.max(me - 1, 0), lax.min(me + 1, n - 1)
    steps = ITERS + 1
    inner = max(d for d in range(1, n + 1) if n % d == 0 and d * d <= n)
    outer = n // inner
    place, group = lax.rem(me, inner), lax.div(me, inner)

    def near(j):
        return group * inner + lax.rem(place + j, inner)

    def far(j):
        return lax.rem(group + j, outer) * inner + place

    loads = [pltpu.make_async_copy(start, top, load_sem.at[0]),
             pltpu.make_async_copy(hop_ops, hop_in, load_sem.at[1])]
    for s in range(count):
        loads.append(pltpu.make_async_copy(left_env.at[s], left_in.at[s], load_sem.at[2 + 2 * s]))
        loads.append(pltpu.make_async_copy(right_env.at[s], right_in.at[s], load_sem.at[3 + 2 * s]))
    for load in loads:
        load.start()

    barrier = pltpu.get_barrier_semaphore()
    left_apart = (place == 0) & has_left
    right_apart = (place == inner - 1) & has_right

    def greet(device):
        pl.semaphore_signal(barrier, inc=1, device_id={"sec": device}, device_id_type=MESH)

    for j in range(1, inner):
        greet(near(j))
    for j in range(1, outer):
        greet(far(j))

    @pl.when(left_apart)
    def _():
        greet(left)

    @pl.when(right_apart)
    def _():
        greet(right)

    rows = lax.broadcasted_iota(jnp.int32, (size, size), 0)
    cols = lax.broadcasted_iota(jnp.int32, (size, size), 1)
    lane = lax.broadcasted_iota(jnp.int32, (1, size), 1)

    def masked(s, x):
        return jnp.where((rows < left_dims[s]) & (cols < right_dims[s]), x, 0.0)

    halo_top[...] = jnp.zeros_like(halo_top)
    cur[...] = jnp.zeros_like(cur)
    img[...] = jnp.zeros_like(img)

    @pl.when(jnp.logical_not(has_left))
    def _():
        rim[...] = jnp.zeros_like(rim)
        for p in range(steps):
            halo_in[p, 0:2] = jnp.zeros((2, size, size), f32)

    @pl.when(jnp.logical_not(has_right))
    def _():
        for p in range(steps):
            halo_in[p, 2:4] = jnp.zeros((2, size, size), f32)

    scale = 1.0 / (6.0 * math.sqrt(count * n * size * size))
    loads[0].wait()
    for s in range(count):
        top[s] = masked(s, top[s]) * scale

    pl.semaphore_wait(
        barrier, inner + outer - 2 + left_apart.astype(jnp.int32) + right_apart.astype(jnp.int32))

    def halo_copy(src, p, s, slot):
        device = right if slot < 2 else left
        return pltpu.make_async_remote_copy(
            src_ref=src.at[s], dst_ref=halo_in.at[p, slot],
            send_sem=halo_send.at[p, slot], recv_sem=halo_recv.at[p, slot],
            device_id={"sec": device}, device_id_type=MESH)

    targets = {}
    for i in range(2):
        targets.setdefault(count - 2 + i, []).append(i)
        targets.setdefault(i, []).append(2 + i)

    def halo_start(src, p, s, more=True):
        for slot in targets.get(s, ()):
            @pl.when((has_right if slot < 2 else has_left) & more)
            def _():
                halo_copy(src, p, s, slot).start()

    def halo_wait(p):
        for s in targets:
            for slot in targets[s]:
                @pl.when(has_right if slot < 2 else has_left)
                def _():
                    halo_copy(out, p, s, slot).wait_send()

                @pl.when(has_left if slot < 2 else has_right)
                def _():
                    halo_copy(out, p, s, slot).wait_recv()

    for s in range(count):
        halo_start(top, 0, s)
    rim_copies = [
        pltpu.make_async_remote_copy(
            src_ref=src, dst_ref=dst, send_sem=rim_send.at[i], recv_sem=rim_recv.at[i],
            device_id={"sec": right}, device_id_type=MESH)
        for i, (src, dst) in enumerate((
            (hop_ops.at[count - 1], rim.at[1]),
            (hop_ops.at[count - 2, 2:4], rim.at[0, 2:4])))]

    @pl.when(has_right)
    def _():
        for copy in rim_copies:
            copy.start()

    def sum_send_all(buffer, which, p, mine, partners):
        for j, device in enumerate(partners):
            pltpu.make_async_remote_copy(
                src_ref=buffer.at[p, mine], dst_ref=buffer.at[p, mine],
                send_sem=sum_send.at[which, p], recv_sem=sum_recv.at[which, p],
                device_id={"sec": device}, device_id_type=MESH).start()

    def sum_wait_all(buffer, which, p, peers):
        if peers == 1:
            return
        whole = buffer.at[p, 0:peers - 1]
        pltpu.make_async_copy(whole, whole, sum_recv.at[which, p]).wait()
        pltpu.make_async_copy(whole, whole, sum_send.at[which, p]).wait()

    def sum_start(p, values):
        line = jnp.zeros((1, size), f32)
        for i, value in enumerate(values):
            line = jnp.where(lane == i, jnp.sum(value, axis=(0, 1), keepdims=True), line)
        sums[p, place] = line
        sum_send_all(sums, 0, p, place, [near(j) for j in range(1, inner)])

    def sum_middle(p):
        sum_wait_all(sums, 0, p, inner)
        tops[p, group] = jnp.sum(sums[p], axis=0)
        sum_send_all(tops, 1, p, group, [far(j) for j in range(1, outer)])

    def sum_end(p):
        sum_wait_all(tops, 1, p, outer)
        line = jnp.sum(tops[p], axis=0)
        return [jnp.broadcast_to(jnp.sum(jnp.where(lane == i, line, 0.0), axis=1, keepdims=True), (1, size))
                for i in range(4)]

    def put(ref, index, row, x):
        hi, lo = halves(x)
        ref[index, row * size:(row + 1) * size, 0:size] = hi
        ref[index, row * size:(row + 1) * size, size:2 * size] = lo

    hop_rows = [[] for _ in range(count)]
    halo_rows = [[] for _ in range(4)]
    seconds = [[] for _ in range(count)]
    own_columns = []
    for s in range(count):
        column = terms
        for inside in (True, False):
            for k in (1, 2):
                for t, owner, flip in ((s + k, s, False), (s - k, s - k, True)):
                    if (0 <= t < count) != inside:
                        continue
                    entry = (s, column, owner, k, flip)
                    if inside:
                        hop_rows[t].append(entry)
                    else:
                        halo_rows[2 + t if t < 0 else 2 + t - count].append(entry)
                    seconds[s].append(entry)
                    column += 1
            if inside:
                own_columns.append(column)

    def hop(owner, index, flip):
        block = hop_in[owner, index] if owner >= 0 else rim[2 + owner, index]
        return block.T if flip else block

    loads[1].wait()
    for s in range(count):
        loads[2 + 2 * s].wait()
        for w in range(terms):
            put(ops_left, s, w, left_in[s, w])
        for i, (_, _, owner, k, flip) in enumerate(hop_rows[s]):
            put(ops_left, s, terms + i, hop(owner, 2 * k - 2, flip))
    for s in range(count):
        loads[3 + 2 * s].wait()
        for w in range(terms):
            put(ops_right, s, w, right_in[s, w])
        for _, column, owner, k, flip in seconds[s]:
            if owner >= 0:
                put(ops_right, s, column, hop(owner, 2 * k - 1, flip))
    for slot in range(4):
        for i, (_, _, owner, k, flip) in enumerate(halo_rows[slot]):
            if owner >= 0:
                put(ops_halo, slot, i, hop(owner, 2 * k - 2, flip))

    def rim_end():
        @pl.when(has_left)
        def _():
            for copy in rim_copies:
                copy.wait_recv()

        @pl.when(has_right)
        def _():
            for copy in rim_copies:
                copy.wait_send()

        for slot in range(4):
            for i, (_, _, owner, k, flip) in enumerate(halo_rows[slot]):
                if owner < 0:
                    put(ops_halo, slot, i, hop(owner, 2 * k - 2, flip))
        for s in range(count):
            for _, column, owner, k, flip in seconds[s]:
                if owner < 0:
                    put(ops_right, s, column, hop(owner, 2 * k - 1, flip))

    def first_stage(ops, index, x, targets_of):
        hi, lo = halves(x)
        line = jnp.concatenate([hi, lo], axis=1)
        both = jnp.concatenate([line, line], axis=0)
        chunk = 4
        for base in range(0, len(targets_of), chunk):
            some = targets_of[base:base + chunk]
            product = jnp.dot(ops[index, base * size:(base + len(some)) * size, :], both,
                              preferred_element_type=f32)
            for i, (s, column) in enumerate(some):
                y = product[i * size:(i + 1) * size]
                hi, lo = halves(y[:, :size] + y[:, size:])
                middle[s, 0:size, column * size:(column + 1) * size] = hi
                middle[s, size:2 * size, column * size:(column + 1) * size] = lo

    def second_stage(s, begin, end):
        product = jnp.dot(middle[s, :, begin * size:end * size], ops_right[s, begin * size:end * size, :],
                          preferred_element_type=f32)
        product = product[:size] + product[size:]
        return product[:, :size] + product[:, size:]

    order = []
    for s in range((count + 1) // 2):
        order += [s] if s == count - 1 - s else [s, count - 1 - s]

    def sums_of(rayleigh):
        values = [jnp.zeros((size, size), f32) for _ in range(4)]
        for s in range(count):
            residual = img[s] - rayleigh * cur[s]
            bent = top[s] - rayleigh * img[s]
            values[0] += residual * residual
            values[1] += residual * bent
            values[2] += cur[s] * bent
            values[3] += residual * img[s]
        return values

    def solve(first, rayleigh, values):
        res_sum, res_bent, cur_bent, res_img = values
        res_sq = res_sum + EPSILON
        res_norm = jnp.sqrt(res_sq)
        curvature = res_bent / res_sq
        lowest = (rayleigh + curvature) / 2 - jnp.sqrt(((rayleigh - curvature) / 2) ** 2 + res_norm * res_norm)
        slope = lowest - rayleigh
        length = jnp.sqrt(res_norm * res_norm + slope * slope)
        keep = jnp.where(first, 0.0, res_norm / length)
        move = jnp.where(first, lax.rsqrt(res_sum), slope / length / res_norm)
        following = keep * keep * rayleigh + keep * move * (cur_bent + res_img) + move * move * res_bent
        return keep, move, lowest, following

    def step(p, carry):
        keep, move, before, rayleigh = [coef[i:i + 1] for i in range(4)]
        sum_start(p, sums_of(rayleigh))
        for t in range(count):
            first_stage(ops_left, t, top[t],
                        [(t, w) for w in range(terms)] + [(e[0], e[1]) for e in hop_rows[t]])
        sum_middle(p)
        for s in order:
            own[s] = second_stage(s, 0, own_columns[s])

        @pl.when(p == 0)
        def _():
            rim_end()

        halo_wait(p)
        for slot in range(4):
            halo_top[slot] = keep * halo_top[slot] + move * (halo_in[p, slot] - before * halo_top[slot])
            first_stage(ops_halo, slot, halo_top[slot], [(e[0], e[1]) for e in halo_rows[slot]])
        for s in order:
            total = own[s]
            if own_columns[s] < terms + 4:
                total = total + second_stage(s, own_columns[s], terms + 4)
            out[s] = masked(s, total)
            halo_start(out, p + 1, s, p < ITERS)

        keep, move, _, following = solve(p == 1, rayleigh, sum_end(p))
        initial = p == 0
        keep = jnp.where(initial, 0.0, keep)
        move = jnp.where(initial, 1.0, move)
        following = jnp.where(initial, 0.0, following)
        for s in range(count):
            cur[s] = keep * cur[s] + move * (img[s] - rayleigh * cur[s])
            img[s] = keep * img[s] + move * (top[s] - rayleigh * img[s])
            top[s] = keep * top[s] + move * (out[s] - rayleigh * top[s])
        for i, value in enumerate((keep, move, rayleigh, following)):
            coef[i:i + 1] = value
        return carry

    nothing = jnp.zeros((1, size), f32)
    for i, value in enumerate((nothing, nothing + 1.0, nothing, nothing)):
        coef[i:i + 1] = value
    lax.fori_loop(0, steps, step, 0)
    rayleigh = coef[3:4]
    sum_start(steps, sums_of(rayleigh))
    sum_middle(steps)
    keep, move, lowest, _ = solve(False, rayleigh, sum_end(steps))
    energy[...] = lowest[:, 0:1]
    for s in range(count):
        ritz[s] = keep * cur[s] + move * (img[s] - rayleigh * cur[s])


def on_device(left_env, right_env, hop_ops, start, left_dims, right_dims):
    count, terms, size = left_env.shape[0], left_env.shape[1], left_env.shape[2]
    n = lax.axis_size("sec")
    blocks = terms + 4
    steps = ITERS + 1
    inner = max(d for d in range(1, n + 1) if n % d == 0 and d * d <= n)
    dma = pltpu.SemaphoreType.DMA
    anywhere = pl.BlockSpec(memory_space=pl.ANY)
    scalars = pl.BlockSpec(memory_space=pltpu.SMEM)
    inside = pl.BlockSpec(memory_space=pltpu.VMEM)
    ritz, energy = pl.pallas_call(
        functools.partial(kernel, n, count, terms),
        out_shape=(jax.ShapeDtypeStruct((count, size, size), f32), jax.ShapeDtypeStruct((1, 1), f32)),
        in_specs=[anywhere] * 4 + [scalars] * 2,
        out_specs=(inside, inside),
        scratch_shapes=[
            pltpu.VMEM((count, terms, size, size), f32),
            pltpu.VMEM((count, terms, size, size), f32),
            pltpu.VMEM((count, 4, size, size), f32),
            pltpu.VMEM((2, 4, size, size), f32),
            pltpu.VMEM((count, blocks * size, 2 * size), bf16),
            pltpu.VMEM((count, blocks * size, 2 * size), bf16),
            pltpu.VMEM((4, 2 * size, 2 * size), bf16),
            pltpu.VMEM((count, 2 * size, blocks * size), bf16),
            pltpu.VMEM((count, size, size), f32),
            pltpu.VMEM((count, size, size), f32),
            pltpu.VMEM((count, size, size), f32),
            pltpu.VMEM((count, size, size), f32),
            pltpu.VMEM((count, size, size), f32),
            pltpu.VMEM((steps, 4, size, size), f32),
            pltpu.VMEM((4, size, size), f32),
            pltpu.VMEM((steps + 1, inner, 1, size), f32),
            pltpu.VMEM((steps + 1, n // inner, 1, size), f32),
            pltpu.VMEM((8, size), f32),
            dma((2 + 2 * count,)),
            dma((2,)), dma((2,)),
            dma((steps, 4)), dma((steps, 4)),
            dma((2, steps + 1)), dma((2, steps + 1)),
        ],
        compiler_params=pltpu.CompilerParams(
            collective_id=0, has_side_effects=True, vmem_limit_bytes=60 * 1024 * 1024),
    )(left_env, right_env, hop_ops, start, left_dims, right_dims)
    total_entries = count * n * size * size
    return ritz * jnp.sqrt(jnp.float32(total_entries)), jnp.reshape(energy, (1,))


def solution(mesh):
    in_specs = (
        P(("parts", "sec"), None, None, None),
        P(("parts", "sec"), None, None, None),
        P(("parts", "sec"), None, None, None),
        P(("parts", "sec"), None, None),
        P(("parts", "sec")),
        P(("parts", "sec")),
    )
    out_specs = (P(("parts", "sec"), None, None), P("parts"))
    return jax.shard_map(
        on_device, mesh=mesh, in_specs=in_specs, out_specs=out_specs, check_vma=False
    )
```

time: 71.8 us -> 56.3 us (0.78)
  Pallas kernels: 63 us -> 52.1 us
  local copies, waits for them, and re-layouts: 5.44 us -> 0 us
  other arithmetic: 0.72 us -> 1.67 us
    pallas_call x1, Pallas kernels: 63 us -> 52.1 us  [on_device(): pl.pallas_call(functools.partial(kernel, n, count, terms), out_shape=(jax...]
    unnamed x10 -> x0, local copies, waits for them, and re-layouts: 5.44 us -> none
    mul x1, other arithmetic: 0.72 us -> 1.67 us  [on_device(): ritz * jnp.sqrt(jnp.float32(total_entries))]
where the time goes in v2:
time: 56.3 us; the launch traced here: 56.1 us
  Pallas kernels  52.1 us (93%)
  between operations  2.4 us (4%)
  other arithmetic  1.67 us (3%)
    pallas_call x1, Pallas kernels, on_device(): pl.pallas_call(functools.partial(kernel, n, count, terms), out_shape=(jax...  52.1 us
    mul x1, other arithmetic, on_device(): ritz * jnp.sqrt(jnp.float32(total_entries))  1.67 us

profile of v2, /device:TPU:0, one launch (start us, length us, event | category | flops | bytes accessed | tf_op | source)
XLA Modules:
  0.0 56.1 jit_solution(10824845336351430299)
XLA Ops:
  0.6 52.1 %shard_map.77 = (f32[4,128,128]{2,1,0:T(8,128)}, f32[1,1]{1,0:T(1,128)}) custom-call(f32[4,13,128,128]{3,2,1,0:T(8,128)} %left_env.1, f32[4,13,128,128]{3,2,1,0:T(8,128)} %right_env.1, f32[4,4,128,128]{3,2,1,0:T(8,128)} %hop_ops.1, f32[4,128,128]{2,1,0:T(8,128)} %start.1, s32[4]{0:T(128)} %left_dims.1, s32[4]{0:T(128)} %right_dims.1), custom_call_target="tpu_custom_call" | custom-call | tf_op jit(solution)/shard_map/pallas_call | solution.py:359
  52.7 1.7 %broadcast_multiply_fusion = f32[4,128,128]{2,1,0:T(8,128)} fusion(f32[4,128,128]{2,1,0:T(8,128)} %get-tuple-element.4), kind=kLoop, calls=%fused_computation | loop fusion | flops 65536 | bytes 524288 | tf_op jit(solution)/shard_map/mul | solution.py:392

commit v3 on v2

--- a/solution.py
+++ b/solution.py
@@ -25,7 +25,7 @@
     left_env, right_env, hop_ops, start, left_dims, right_dims,
     ritz, energy,
     left_in, right_in, hop_in, rim, ops_left, ops_right, ops_halo, middle,
-    cur, img, top, own, out, halo_in, halo_top, sums, tops, coef,
+    cur, img, top, own, out, halo_in, halo_top, sums, coef,
     load_sem, rim_send, rim_recv, halo_send, halo_recv, sum_send, sum_recv,
 ):
     size = start.shape[1]
@@ -33,43 +33,20 @@
     has_left, has_right = me > 0, me < n - 1
     left, right = lax.max(me - 1, 0), lax.min(me + 1, n - 1)
     steps = ITERS + 1
-    inner = max(d for d in range(1, n + 1) if n % d == 0 and d * d <= n)
-    outer = n // inner
-    place, group = lax.rem(me, inner), lax.div(me, inner)
-
-    def near(j):
-        return group * inner + lax.rem(place + j, inner)
-
-    def far(j):
-        return lax.rem(group + j, outer) * inner + place
+    peers = [lax.rem(me + j, n) for j in range(1, n)]
 
     loads = [pltpu.make_async_copy(start, top, load_sem.at[0]),
              pltpu.make_async_copy(hop_ops, hop_in, load_sem.at[1])]
     for s in range(count):
-        loads.append(pltpu.make_async_copy(left_env.at[s], left_in.at[s], load_sem.at[2 + 2 * s]))
-        loads.append(pltpu.make_async_copy(right_env.at[s], right_in.at[s], load_sem.at[3 + 2 * s]))
+        loads.append(pltpu.make_async_copy(left_env.at[s], left_in.at[s], load_sem.at[2 + s]))
+    for s in range(count):
+        loads.append(pltpu.make_async_copy(right_env.at[s], right_in.at[s], load_sem.at[2 + count + s]))
     for load in loads:
         load.start()
 
     barrier = pltpu.get_barrier_semaphore()
-    left_apart = (place == 0) & has_left
-    right_apart = (place == inner - 1) & has_right
-
-    def greet(device):
+    for device in peers:
         pl.semaphore_signal(barrier, inc=1, device_id={"sec": device}, device_id_type=MESH)
-
-    for j in range(1, inner):
-        greet(near(j))
-    for j in range(1, outer):
-        greet(far(j))
-
-    @pl.when(left_apart)
-    def _():
-        greet(left)
-
-    @pl.when(right_apart)
-    def _():
-        greet(right)
 
     rows = lax.broadcasted_iota(jnp.int32, (size, size), 0)
     cols = lax.broadcasted_iota(jnp.int32, (size, size), 1)
@@ -97,9 +74,6 @@
     loads[0].wait()
     for s in range(count):
         top[s] = masked(s, top[s]) * scale
-
-    pl.semaphore_wait(
-        barrier, inner + outer - 2 + left_apart.astype(jnp.int32) + right_apart.astype(jnp.int32))
 
     def halo_copy(src, p, s, slot):
         device = right if slot < 2 else left
@@ -130,50 +104,23 @@
                 def _():
                     halo_copy(out, p, s, slot).wait_recv()
 
-    for s in range(count):
-        halo_start(top, 0, s)
-    rim_copies = [
-        pltpu.make_async_remote_copy(
-            src_ref=src, dst_ref=dst, send_sem=rim_send.at[i], recv_sem=rim_recv.at[i],
-            device_id={"sec": right}, device_id_type=MESH)
-        for i, (src, dst) in enumerate((
-            (hop_ops.at[count - 1], rim.at[1]),
-            (hop_ops.at[count - 2, 2:4], rim.at[0, 2:4])))]
-
-    @pl.when(has_right)
-    def _():
-        for copy in rim_copies:
-            copy.start()
-
-    def sum_send_all(buffer, which, p, mine, partners):
-        for j, device in enumerate(partners):
-            pltpu.make_async_remote_copy(
-                src_ref=buffer.at[p, mine], dst_ref=buffer.at[p, mine],
-                send_sem=sum_send.at[which, p], recv_sem=sum_recv.at[which, p],
-                device_id={"sec": device}, device_id_type=MESH).start()
-
-    def sum_wait_all(buffer, which, p, peers):
-        if peers == 1:
-            return
-        whole = buffer.at[p, 0:peers - 1]
-        pltpu.make_async_copy(whole, whole, sum_recv.at[which, p]).wait()
-        pltpu.make_async_copy(whole, whole, sum_send.at[which, p]).wait()
-
     def sum_start(p, values):
         line = jnp.zeros((1, size), f32)
         for i, value in enumerate(values):
             line = jnp.where(lane == i, jnp.sum(value, axis=(0, 1), keepdims=True), line)
-        sums[p, place] = line
-        sum_send_all(sums, 0, p, place, [near(j) for j in range(1, inner)])
-
-    def sum_middle(p):
-        sum_wait_all(sums, 0, p, inner)
-        tops[p, group] = jnp.sum(sums[p], axis=0)
-        sum_send_all(tops, 1, p, group, [far(j) for j in range(1, outer)])
+        sums[p, me] = line
+        for device in peers:
+            pltpu.make_async_remote_copy(
+                src_ref=sums.at[p, me], dst_ref=sums.at[p, me],
+                send_sem=sum_send.at[p], recv_sem=sum_recv.at[p],
+                device_id={"sec": device}, device_id_type=MESH).start()
 
     def sum_end(p):
-        sum_wait_all(tops, 1, p, outer)
-        line = jnp.sum(tops[p], axis=0)
+        if n > 1:
+            whole = sums.at[p, 0:n - 1]
+            pltpu.make_async_copy(whole, whole, sum_recv.at[p]).wait()
+            pltpu.make_async_copy(whole, whole, sum_send.at[p]).wait()
+        line = jnp.sum(sums[p], axis=0)
         return [jnp.broadcast_to(jnp.sum(jnp.where(lane == i, line, 0.0), axis=1, keepdims=True), (1, size))
                 for i in range(4)]
 
@@ -209,13 +156,29 @@
 
     loads[1].wait()
     for s in range(count):
-        loads[2 + 2 * s].wait()
+        loads[2 + s].wait()
         for w in range(terms):
             put(ops_left, s, w, left_in[s, w])
         for i, (_, _, owner, k, flip) in enumerate(hop_rows[s]):
             put(ops_left, s, terms + i, hop(owner, 2 * k - 2, flip))
-    for s in range(count):
-        loads[3 + 2 * s].wait()
+    pl.semaphore_wait(barrier, n - 1)
+    for s in range(count):
+        halo_start(top, 0, s)
+    rim_copies = [
+        pltpu.make_async_remote_copy(
+            src_ref=src, dst_ref=dst, send_sem=rim_send.at[i], recv_sem=rim_recv.at[i],
+            device_id={"sec": right}, device_id_type=MESH)
+        for i, (src, dst) in enumerate((
+            (hop_ops.at[count - 1], rim.at[1]),
+            (hop_ops.at[count - 2, 2:4], rim.at[0, 2:4])))]
+
+    @pl.when(has_right)
+    def _():
+        for copy in rim_copies:
+            copy.start()
+
+    for s in range(count):
+        loads[2 + count + s].wait()
         for w in range(terms):
             put(ops_right, s, w, right_in[s, w])
         for _, column, owner, k, flip in seconds[s]:
@@ -301,7 +264,6 @@
         for t in range(count):
             first_stage(ops_left, t, top[t],
                         [(t, w) for w in range(terms)] + [(e[0], e[1]) for e in hop_rows[t]])
-        sum_middle(p)
         for s in order:
             own[s] = second_stage(s, 0, own_columns[s])
 
@@ -339,7 +301,6 @@
     lax.fori_loop(0, steps, step, 0)
     rayleigh = coef[3:4]
     sum_start(steps, sums_of(rayleigh))
-    sum_middle(steps)
     keep, move, lowest, _ = solve(False, rayleigh, sum_end(steps))
     energy[...] = lowest[:, 0:1]
     for s in range(count):
@@ -351,7 +312,6 @@
     n = lax.axis_size("sec")
     blocks = terms + 4
     steps = ITERS + 1
-    inner = max(d for d in range(1, n + 1) if n % d == 0 and d * d <= n)
     dma = pltpu.SemaphoreType.DMA
     anywhere = pl.BlockSpec(memory_space=pl.ANY)
     scalars = pl.BlockSpec(memory_space=pltpu.SMEM)
@@ -377,13 +337,12 @@
             pltpu.VMEM((count, size, size), f32),
             pltpu.VMEM((steps, 4, size, size), f32),
             pltpu.VMEM((4, size, size), f32),
-            pltpu.VMEM((steps + 1, inner, 1, size), f32),
-            pltpu.VMEM((steps + 1, n // inner, 1, size), f32),
+            pltpu.VMEM((steps + 1, n, 1, size), f32),
             pltpu.VMEM((8, size), f32),
             dma((2 + 2 * count,)),
             dma((2,)), dma((2,)),
             dma((steps, 4)), dma((steps, 4)),
-            dma((2, steps + 1)), dma((2, steps + 1)),
+            dma((steps + 1,)), dma((steps + 1,)),
         ],
         compiler_params=pltpu.CompilerParams(
             collective_id=0, has_side_effects=True, vmem_limit_bytes=60 * 1024 * 1024),

time: 56.3 us -> 45.5 us (0.81)
  Pallas kernels: 52.1 us -> 41.3 us
    pallas_call x1, Pallas kernels: 52.1 us -> 41.3 us  [on_device(): pl.pallas_call(functools.partial(kernel, n, count, terms), out_shape=(jax...]
where the time goes in v3:
time: 45.5 us; the launch traced here: 45.3 us
  Pallas kernels  41.3 us (91%)
  between operations  2.4 us (5%)
  other arithmetic  1.67 us (4%)
    pallas_call x1, Pallas kernels, on_device(): pl.pallas_call(functools.partial(kernel, n, count, terms), out_shape=(jax...  41.3 us
    mul x1, other arithmetic, on_device(): ritz * jnp.sqrt(jnp.float32(total_entries))  1.67 us

profile of v3, /device:TPU:0, one launch (start us, length us, event | category | flops | bytes accessed | tf_op | source)
XLA Modules:
  0.0 45.3 jit_solution(15929049864373575840)
XLA Ops:
  0.6 41.3 %shard_map.77 = (f32[4,128,128]{2,1,0:T(8,128)}, f32[1,1]{1,0:T(1,128)}) custom-call(f32[4,13,128,128]{3,2,1,0:T(8,128)} %left_env.1, f32[4,13,128,128]{3,2,1,0:T(8,128)} %right_env.1, f32[4,4,128,128]{3,2,1,0:T(8,128)} %hop_ops.1, f32[4,128,128]{2,1,0:T(8,128)} %start.1, s32[4]{0:T(128)} %left_dims.1, s32[4]{0:T(128)} %right_dims.1), custom_call_target="tpu_custom_call" | custom-call | tf_op jit(solution)/shard_map/pallas_call | solution.py:319
  41.9 1.7 %broadcast_multiply_fusion = f32[4,128,128]{2,1,0:T(8,128)} fusion(f32[4,128,128]{2,1,0:T(8,128)} %get-tuple-element.4), kind=kLoop, calls=%fused_computation | loop fusion | flops 65536 | bytes 524288 | tf_op jit(solution)/shard_map/mul | solution.py:351

commit v4 on v3

--- a/solution.py
+++ b/solution.py
@@ -35,6 +35,10 @@
     steps = ITERS + 1
     peers = [lax.rem(me + j, n) for j in range(1, n)]
 
+    barrier = pltpu.get_barrier_semaphore()
+    for device in peers:
+        pl.semaphore_signal(barrier, inc=1, device_id={"sec": device}, device_id_type=MESH)
+
     loads = [pltpu.make_async_copy(start, top, load_sem.at[0]),
              pltpu.make_async_copy(hop_ops, hop_in, load_sem.at[1])]
     for s in range(count):
@@ -44,10 +48,6 @@
     for load in loads:
         load.start()
 
-    barrier = pltpu.get_barrier_semaphore()
-    for device in peers:
-        pl.semaphore_signal(barrier, inc=1, device_id={"sec": device}, device_id_type=MESH)
-
     rows = lax.broadcasted_iota(jnp.int32, (size, size), 0)
     cols = lax.broadcasted_iota(jnp.int32, (size, size), 1)
     lane = lax.broadcasted_iota(jnp.int32, (1, size), 1)
@@ -58,6 +58,7 @@
     halo_top[...] = jnp.zeros_like(halo_top)
     cur[...] = jnp.zeros_like(cur)
     img[...] = jnp.zeros_like(img)
+    sums[0] = jnp.zeros((n, 1, size), f32)
 
     @pl.when(jnp.logical_not(has_left))
     def _():
@@ -117,9 +118,12 @@
 
     def sum_end(p):
         if n > 1:
-            whole = sums.at[p, 0:n - 1]
-            pltpu.make_async_copy(whole, whole, sum_recv.at[p]).wait()
-            pltpu.make_async_copy(whole, whole, sum_send.at[p]).wait()
+            @pl.when(p > 0)
+            def _():
+                whole = sums.at[p, 0:n - 1]
+                pltpu.make_async_copy(whole, whole, sum_recv.at[p]).wait()
+                pltpu.make_async_copy(whole, whole, sum_send.at[p]).wait()
+
         line = jnp.sum(sums[p], axis=0)
         return [jnp.broadcast_to(jnp.sum(jnp.where(lane == i, line, 0.0), axis=1, keepdims=True), (1, size))
                 for i in range(4)]
@@ -260,7 +264,10 @@
 
     def step(p, carry):
         keep, move, before, rayleigh = [coef[i:i + 1] for i in range(4)]
-        sum_start(p, sums_of(rayleigh))
+        @pl.when(p > 0)
+        def _():
+            sum_start(p, sums_of(rayleigh))
+
         for t in range(count):
             first_stage(ops_left, t, top[t],
                         [(t, w) for w in range(terms)] + [(e[0], e[1]) for e in hop_rows[t]])

time: 45.5 us -> 45.5 us (level)
  no operation moved by 1% of the time
where the time goes in v4:
time: 45.5 us; the launch traced here: 45.3 us
  Pallas kernels  41.2 us (91%)
  between operations  2.4 us (5%)
  other arithmetic  1.67 us (4%)
    pallas_call x1, Pallas kernels, on_device(): pl.pallas_call(functools.partial(kernel, n, count, terms), out_shape=(jax...  41.2 us
    mul x1, other arithmetic, on_device(): ritz * jnp.sqrt(jnp.float32(total_entries))  1.67 us

profile of v4, /device:TPU:0, one launch (start us, length us, event | category | flops | bytes accessed | tf_op | source)
XLA Modules:
  0.0 45.3 jit_solution(12451802624635413548)
XLA Ops:
  0.6 41.2 %shard_map.77 = (f32[4,128,128]{2,1,0:T(8,128)}, f32[1,1]{1,0:T(1,128)}) custom-call(f32[4,13,128,128]{3,2,1,0:T(8,128)} %left_env.1, f32[4,13,128,128]{3,2,1,0:T(8,128)} %right_env.1, f32[4,4,128,128]{3,2,1,0:T(8,128)} %hop_ops.1, f32[4,128,128]{2,1,0:T(8,128)} %start.1, s32[4]{0:T(128)} %left_dims.1, s32[4]{0:T(128)} %right_dims.1), custom_call_target="tpu_custom_call" | custom-call | tf_op jit(solution)/shard_map/pallas_call | solution.py:326
  41.8 1.7 %broadcast_multiply_fusion = f32[4,128,128]{2,1,0:T(8,128)} fusion(f32[4,128,128]{2,1,0:T(8,128)} %get-tuple-element.4), kind=kLoop, calls=%fused_computation | loop fusion | flops 65536 | bytes 524288 | tf_op jit(solution)/shard_map/mul | solution.py:358
